TPU v7x, 256 devices: a whole 4x4x8 slice. The times are simulated.
256 devices in a mesh: noise: 8 (over x, core), sample: 32 (over y, z).
Axes of the slice: x: 4, y: 4, z: 8, core: 2. Of those that a mesh axis runs over, the one named last changes fastest.
Arguments:
- noise_latents: bfloat16 [16384, 256], P(('noise', 'sample')), may hold values from -18 to 18
- teacher_latent_rows: bfloat16 [32768, 256], P('sample', 'noise'), may hold values from -6 to 6
Outputs:
- noise_row_potential: float32 [16384], P('noise')
- column_potential: float32 [32768], P('sample')
- targets: bfloat16 [16384, 256], P(('noise', 'sample'))
All inputs are finite; a program needn't handle non-finite values.
Results may differ from a plain program's by a relative error of at most 0.0039.
Values may be sent and summed in bfloat16 or wider, within the bound.
A program may use at most 64 MiB of HBM per device.

v0:
```python
import math
import jax
import jax.numpy as jnp
from jax import lax
from jax.sharding import PartitionSpec as P

ITERS = 3
smoothing_strength = 0.1


def source_logsumexp_partial(scores):
    local_peak = jnp.max(scores, axis=1)
    peak = lax.pmax(local_peak, "sample")
    total = lax.psum(jnp.sum(jnp.exp(scores - peak[:, None]), axis=1), "sample")
    return peak + jnp.log(total)


def col_lse(scores):
    local_peak = jnp.max(scores, axis=0)
    peak = lax.pmax(local_peak, "noise")
    total = lax.psum(jnp.sum(jnp.exp(scores - peak[None, :]), axis=0), "noise")
    return peak + jnp.log(total)


def shards(noise_latents, teacher_latent_rows):
    rows_x = lax.all_gather(noise_latents, "sample", axis=0, tiled=True)
    cols_y = lax.all_gather(teacher_latent_rows, "noise", axis=1, tiled=True)
    embed_dimension = rows_x.shape[1]
    multiplier_coefficient = 1.0 / (embed_dimension * smoothing_strength)
    row_count = rows_x.shape[0]
    col_count = cols_y.shape[0]
    total_rows = row_count * lax.axis_size("noise")
    overall_destination_number = col_count * lax.axis_size("sample")
    xn = jnp.sum(rows_x.astype(jnp.float32) ** 2, axis=1)
    yn = jnp.sum(cols_y.astype(jnp.float32) ** 2, axis=1)

    def kernel():
        inner = jnp.dot(rows_x, cols_y.T, preferred_element_type=jnp.float32)
        return (xn[:, None] + yn[None, :] - 2.0 * inner) * multiplier_coefficient

    def cost():
        return kernel()

    column_potential = jnp.zeros((col_count,), jnp.float32)
    noise_row_potential = jnp.zeros((row_count,), jnp.float32)
    for step in range(ITERS):
        noise_row_potential = -math.log(total_rows) - source_logsumexp_partial(
            column_potential[None, :] - cost()
        )
        column_potential = -math.log(overall_destination_number) - col_lse(
            noise_row_potential[:, None] - cost()
        )
    plan = jnp.exp(noise_row_potential[:, None] + column_potential[None, :] - cost())
    mass_part = jnp.sum(plan, axis=1)
    numer = jnp.dot(plan.astype(jnp.bfloat16), cols_y, preferred_element_type=jnp.float32)
    numer_all, mass_all = lax.psum((numer, mass_part), "sample")
    share = row_count // lax.axis_size("sample")
    start = lax.axis_index("sample") * share
    numer_own = lax.dynamic_slice_in_dim(numer_all, start, share, 0)
    mass_own = lax.dynamic_slice_in_dim(mass_all, start, share, 0)
    targets = (numer_own / mass_own[:, None]).astype(jnp.bfloat16)
    return (noise_row_potential, column_potential, targets)


def solution(mesh):
    placed = (P(("noise", "sample"), None), P("sample", "noise"))
    return jax.shard_map(
        shards,
        mesh=mesh,
        in_specs=placed,
        out_specs=(P("noise"), P("sample"), P(("noise", "sample"), None)),
        check_vma=False,
    )
```

profile of v0, /device:TPU:2, one launch (start us, length us, event | category | flops | bytes accessed | tf_op | source)
XLA Modules:
  0.0 811.2 jit_solution(9159708319463455959)
XLA Ops:
  7.2 0.0 all-gather.2.cloned.1.call-start
  7.2 0.7 all-gather.2.cloned.1.call-update
  7.9 0.0 all-reduce.2.cloned.1.call-start
  7.9 13.4 %all_gather.7 = bf16[1024,256]{0,1:T(8,128)(2,1)S(1)} all-gather(bf16[1024,32]{0,1:T(8,128)(2,1)} %param.3), channel_id=1, replica_groups=mesh['noise'=8,'sample'=32] {'noise'}, dimensions={1}, use_global_device_ids=true | all-gather | bytes 589824 | tf_op jit(solution)/shard_map/all_gather | solution.py:27
  21.3 0.1 multiply_reduce_fusion.1
  21.4 68.3 %all-gather.2.cloned.1.call-done = bf16[2048,256]{1,0:T(8,128)(2,1)} async-done(((bf16[64,256]{1,0:T(8,128)(2,1)}), bf16[2048,256]{1,0:T(8,128)(2,1)}) %all-gather.2.cloned.1.call-update) | async-done | bytes 1048592 | tf_op jit(solution)/shard_map/all_gather | solution.py:26
  89.8 1.6 multiply_reduce_fusion
  91.3 5.6 subtract_reduce_fusion.5
  96.9 73.3 %pmax.42 = f32[2048]{0:T(1024)S(1)} all-reduce(f32[2048]{0:T(1024)S(1)} %get-tuple-element.3), channel_id=1, replica_groups=mesh['noise'=8,'sample'=32] {'sample'}, use_global_device_ids=true, to_apply=%region_3.0 | all-reduce | flops 2048 | bytes 16384 | tf_op jit(solution)/shard_map/pmax | solution.py:13
  170.1 4.8 exponential_reduce_fusion.5
  174.9 70.7 %psum.56 = f32[2048]{0:T(1024)S(1)} all-reduce(f32[2048]{0:T(1024)S(1)} %exponential_reduce_fusion.5), channel_id=1, replica_groups=mesh['noise'=8,'sample'=32] {'sample'}, use_global_device_ids=true, to_apply=%region_5.0 | all-reduce | flops 2048 | bytes 16384 | tf_op jit(solution)/shard_map/psum | solution.py:14
  245.7 4.0 subtract_reduce_fusion.4
  249.7 10.0 %pmax.43 = f32[1024]{0:T(1024)S(1)} all-reduce(f32[1024]{0:T(1024)S(1)} %subtract_reduce_fusion.4), channel_id=1, replica_groups=mesh['noise'=8,'sample'=32] {'noise'}, use_global_device_ids=true, to_apply=%region_7.0 | all-reduce | flops 1024 | bytes 8192 | tf_op jit(solution)/shard_map/pmax | solution.py:20
  259.7 4.4 exponential_reduce_fusion.4
  264.1 12.4 %psum.57 = f32[1024]{0:T(1024)S(1)} all-reduce(f32[1024]{0:T(1024)S(1)} %exponential_reduce_fusion.4), channel_id=1, replica_groups=mesh['noise'=8,'sample'=32] {'noise'}, use_global_device_ids=true, to_apply=%region_9.0 | all-reduce | flops 1024 | bytes 8192 | tf_op jit(solution)/shard_map/psum | solution.py:21
  276.5 4.0 subtract_reduce_fusion.3
  280.6 72.6 %pmax.44 = f32[2048]{0:T(1024)S(1)} all-reduce(f32[2048]{0:T(1024)S(1)} %subtract_reduce_fusion.3), channel_id=1, replica_groups=mesh['noise'=8,'sample'=32] {'sample'}, use_global_device_ids=true, to_apply=%region_11.0 | all-reduce | flops 2048 | bytes 16384 | tf_op jit(solution)/shard_map/pmax | solution.py:13
  353.2 4.3 exponential_reduce_fusion.3
  357.5 70.7 %psum.58 = f32[2048]{0:T(1024)S(1)} all-reduce(f32[2048]{0:T(1024)S(1)} %exponential_reduce_fusion.3), channel_id=1, replica_groups=mesh['noise'=8,'sample'=32] {'sample'}, use_global_device_ids=true, to_apply=%region_13.0 | all-reduce | flops 2048 | bytes 16384 | tf_op jit(solution)/shard_map/psum | solution.py:14
  428.2 4.0 subtract_reduce_fusion.2
  432.2 11.9 %pmax.45 = f32[1024]{0:T(1024)S(1)} all-reduce(f32[1024]{0:T(1024)S(1)} %subtract_reduce_fusion.2), channel_id=1, replica_groups=mesh['noise'=8,'sample'=32] {'noise'}, use_global_device_ids=true, to_apply=%region_15.0 | all-reduce | flops 1024 | bytes 8192 | tf_op jit(solution)/shard_map/pmax | solution.py:20
  444.1 4.4 exponential_reduce_fusion.2
  448.5 12.9 %psum.59 = f32[1024]{0:T(1024)S(1)} all-reduce(f32[1024]{0:T(1024)S(1)} %exponential_reduce_fusion.2), channel_id=1, replica_groups=mesh['noise'=8,'sample'=32] {'noise'}, use_global_device_ids=true, to_apply=%region_17.0 | all-reduce | flops 1024 | bytes 8192 | tf_op jit(solution)/shard_map/psum | solution.py:21
  461.4 4.0 subtract_reduce_fusion.1
  465.4 72.6 %pmax.46 = f32[2048]{0:T(1024)S(1)} all-reduce(f32[2048]{0:T(1024)S(1)} %subtract_reduce_fusion.1), channel_id=1, replica_groups=mesh['noise'=8,'sample'=32] {'sample'}, use_global_device_ids=true, to_apply=%region_19.0 | all-reduce | flops 2048 | bytes 16384 | tf_op jit(solution)/shard_map/pmax | solution.py:13
  538.0 4.3 exponential_reduce_fusion.1
  542.4 70.9 %psum.60 = f32[2048]{0:T(1024)S(1)} all-reduce(f32[2048]{0:T(1024)S(1)} %exponential_reduce_fusion.1), channel_id=1, replica_groups=mesh['noise'=8,'sample'=32] {'sample'}, use_global_device_ids=true, to_apply=%region_21.0 | all-reduce | flops 2048 | bytes 16384 | tf_op jit(solution)/shard_map/psum | solution.py:14
  613.3 0.0 copy-start
  613.3 4.0 subtract_reduce_fusion
  617.3 11.9 %pmax.47 = f32[1024]{0:T(1024)S(1)} all-reduce(f32[1024]{0:T(1024)S(1)} %subtract_reduce_fusion), channel_id=1, replica_groups=mesh['noise'=8,'sample'=32] {'noise'}, use_global_device_ids=true, to_apply=%region_23.0 | all-reduce | flops 1024 | bytes 8192 | tf_op jit(solution)/shard_map/pmax | solution.py:20
  629.2 4.4 exponential_reduce_fusion
  633.6 12.9 %psum.61 = f32[1024]{0:T(1024)S(1)} all-reduce(f32[1024]{0:T(1024)S(1)} %exponential_reduce_fusion), channel_id=1, replica_groups=mesh['noise'=8,'sample'=32] {'noise'}, use_global_device_ids=true, to_apply=%region_25.0 | all-reduce | flops 1024 | bytes 8192 | tf_op jit(solution)/shard_map/psum | solution.py:21
  646.5 0.0 copy-start.1
  646.5 6.5 fusion.2
  653.0 0.0 all-reduce.2.cloned.1.call-update
  653.0 0.0 copy-done
  653.0 0.0 copy-done.1
  653.0 4.3 fusion
  657.3 72.8 %psum.63 = f32[2048]{0:T(1024)S(1)} all-reduce(f32[2048]{0:T(1024)S(1)} %fusion), channel_id=1, replica_groups=mesh['noise'=8,'sample'=32] {'sample'}, use_global_device_ids=true, to_apply=%region_28.0 | all-reduce | flops 2048 | bytes 16384 | tf_op jit(solution)/shard_map/psum | solution.py:56
  730.2 0.1 dynamic_slice.7
  730.3 72.6 %all-reduce.2.cloned.1.call-done = f32[2048,256]{1,0:T(8,128)} async-done(((f32[2048,256]{1,0:T(8,128)}), f32[2048,256]{1,0:T(8,128)}) %all-reduce.2.cloned.1.call-update) | async-done | bytes 2097168 | tf_op jit(solution)/shard_map/psum | solution.py:56
  802.9 1.5 divide_convert_fusion
  (6 shorter events, 0.1 us)
Async XLA Ops:
  7.2 82.6 %all-gather.2.cloned.1.call-start = ((), (), s32[]{:S(2)}) async-start(), calls=%async_computation | async-start | bytes 1081344 | tf_op jit(solution)/shard_map/all_gather | solution.py:26
  7.9 795.0 %all-reduce.2.cloned.1.call-start = ((), (), s32[]{:S(2)}) async-start(), calls=%async_computation.1 | async-start | bytes 4194304 | tf_op jit(solution)/shard_map/psum | solution.py:56
  613.3 39.7 %copy-start = (f32[2048]{0:T(1024)}, f32[2048]{0:T(1024)S(1)}, u32[]{:S(2)}) copy-start(f32[2048]{0:T(1024)S(1)} %add_subtract_fusion) | copy-start | bytes 24580
  646.5 6.5 copy-start.1
Sparse Core Ops, SparseCore 0:
  10.6 79.1 all-gather.1
  653.1 149.6 all-reduce.1
where the time goes:
time: 812 us; the launch traced here: 811 us
  blocking collectives  589 us (73%)
  waiting for transfers between devices  142 us (17%)
  other arithmetic  54.1 us (7%)
  between operations  14.2 us (2%)
  matrix products  12 us (1%)
    pmax x3, blocking collectives, source_logsumexp_partial(): peak = lax.pmax(local_peak, 'sample')  218 us
    psum x3, blocking collectives, source_logsumexp_partial(): total = lax.psum(jnp.sum(jnp.exp(scores - peak[:, None]), axis=1), 'sample')  212 us
    psum x1, blocking collectives, shards(): numer_all, mass_all = lax.psum((numer, mass_part), 'sample')  72.8 us
    psum x1, waiting for transfers between devices, shards(): numer_all, mass_all = lax.psum((numer, mass_part), 'sample')  72.6 us
    all_gather x1, waiting for transfers between devices, shards(): rows_x = lax.all_gather(noise_latents, 'sample', axis=0, tiled=True)  68.3 us
    psum x3, blocking collectives, col_lse(): total = lax.psum(jnp.sum(jnp.exp(scores - peak[None, :]), axis=0), 'noise')  38.3 us
    pmax x3, blocking collectives, col_lse(): peak = lax.pmax(local_peak, 'noise')  33.8 us
  transfers between devices with their start and end apart: 2, of which 2 were waited for; matrix products, arithmetic and copies ran while one was open for 1% of the time, Pallas kernels for 0%

commit v1 on v0

--- a/solution.py
+++ b/solution.py
@@ -23,7 +23,15 @@
 
 
 def shards(noise_latents, teacher_latent_rows):
-    rows_x = lax.all_gather(noise_latents, "sample", axis=0, tiled=True)
+    rows_x = jnp.concatenate(
+        jax.lax.all_to_all(
+            jnp.stack([noise_latents] * jax.lax.axis_size("sample"), 0),
+            axis_name="sample",
+            concat_axis=0,
+            split_axis=0,
+        ),
+        0,
+    )
     cols_y = lax.all_gather(teacher_latent_rows, "noise", axis=1, tiled=True)
     embed_dimension = rows_x.shape[1]
     multiplier_coefficient = 1.0 / (embed_dimension * smoothing_strength)

time: 812 us -> 769 us (0.947)
  waiting for transfers between devices: 142 us -> 87.9 us
  starting transfers between devices: 0.08 us -> 11.5 us
    all_gather x1 -> x0, waiting for transfers between devices: 68.3 us -> none  [shards(): rows_x = lax.all_gather(noise_latents, 'sample', axis=0, tiled=True)]
    all_to_all x0 -> x1, waiting for transfers between devices: none -> 15.1 us  [shards(): jax.lax.all_to_all(jnp.stack([noise_latents] * jax.lax.axis_size('sample'...]
    all_to_all x0 -> x1, starting transfers between devices: none -> 11.5 us  [shards(): jax.lax.all_to_all(jnp.stack([noise_latents] * jax.lax.axis_size('sample'...]
where the time goes in v1:
time: 769 us; the launch traced here: 768 us
  blocking collectives  589 us (77%)
  waiting for transfers between devices  87.9 us (11%)
  other arithmetic  52.9 us (7%)
  between operations  14.2 us (2%)
  starting transfers between devices  11.5 us (1%)
  matrix products  10.8 us (1%)
    pmax x3, blocking collectives, source_logsumexp_partial(): peak = lax.pmax(local_peak, 'sample')  219 us
    psum x3, blocking collectives, source_logsumexp_partial(): total = lax.psum(jnp.sum(jnp.exp(scores - peak[:, None]), axis=1), 'sample')  212 us
    psum x1, blocking collectives, shards(): numer_all, mass_all = lax.psum((numer, mass_part), 'sample')  72.9 us
    psum x1, waiting for transfers between devices, shards(): numer_all, mass_all = lax.psum((numer, mass_part), 'sample')  72.8 us
    psum x3, blocking collectives, col_lse(): total = lax.psum(jnp.sum(jnp.exp(scores - peak[None, :]), axis=0), 'noise')  38.3 us
    pmax x3, blocking collectives, col_lse(): peak = lax.pmax(local_peak, 'noise')  33.7 us
  transfers between devices with their start and end apart: 2, of which 2 were waited for; matrix products, arithmetic and copies ran while one was open for 1% of the time, Pallas kernels for 0%

profile of v1, /device:TPU:2, one launch (start us, length us, event | category | flops | bytes accessed | tf_op | source)
XLA Modules:
  0.0 768.3 jit_solution(16960596037401111321)
XLA Ops:
  7.2 1.9 stack.2
  9.0 11.5 %all-to-all-start = ((bf16[32,64,256]{2,1,0:T(8,128)(2,1)}), bf16[32,64,256]{2,1,0:T(8,128)(2,1)S(1)}, u32[]{:S(2)}, u32[]{:S(2)}) async-start(bf16[32,64,256]{2,1,0:T(8,128)(2,1)} %stack.2), calls=%async_computation | async-start | bytes 2097152 | tf_op jit(solution)/shard_map/all_to_all | solution.py:27
  20.5 0.0 all-reduce.2.cloned.1.call-start
  20.6 13.4 %all_gather.3 = bf16[1024,256]{0,1:T(8,128)(2,1)S(1)} all-gather(bf16[1024,32]{0,1:T(8,128)(2,1)} %param.3), channel_id=1, replica_groups=mesh['noise'=8,'sample'=32] {'noise'}, dimensions={1}, use_global_device_ids=true | all-gather | bytes 589824 | tf_op jit(solution)/shard_map/all_gather | solution.py:35
  34.0 0.1 multiply_reduce_fusion.1
  34.1 15.1 %all-to-all-done = bf16[32,64,256]{2,1,0:T(8,128)(2,1)S(1)} async-done(((bf16[32,64,256]{2,1,0:T(8,128)(2,1)}), bf16[32,64,256]{2,1,0:T(8,128)(2,1)S(1)}, u32[]{:S(2)}, u32[]{:S(2)}) %all-to-all-start) | async-done | bytes 1048608 | tf_op jit(solution)/shard_map/all_to_all | solution.py:27
  49.2 0.3 multiply_reduce_fusion
  49.5 0.1 add.23
  49.6 4.3 subtract_reduce_fusion.5
  53.9 73.0 %pmax.42 = f32[2048]{0:T(1024)S(1)} all-reduce(f32[2048]{0:T(1024)S(1)} %get-tuple-element.3), channel_id=1, replica_groups=mesh['noise'=8,'sample'=32] {'sample'}, use_global_device_ids=true, to_apply=%region_3.0 | all-reduce | flops 2048 | bytes 16384 | tf_op jit(solution)/shard_map/pmax | solution.py:13
  126.9 4.8 exponential_reduce_fusion.5
  131.6 70.6 %psum.56 = f32[2048]{0:T(1024)S(1)} all-reduce(f32[2048]{0:T(1024)S(1)} %exponential_reduce_fusion.5), channel_id=1, replica_groups=mesh['noise'=8,'sample'=32] {'sample'}, use_global_device_ids=true, to_apply=%region_5.0 | all-reduce | flops 2048 | bytes 16384 | tf_op jit(solution)/shard_map/psum | solution.py:14
  202.3 4.0 subtract_reduce_fusion.4
  206.3 10.0 %pmax.43 = f32[1024]{0:T(1024)S(1)} all-reduce(f32[1024]{0:T(1024)S(1)} %subtract_reduce_fusion.4), channel_id=1, replica_groups=mesh['noise'=8,'sample'=32] {'noise'}, use_global_device_ids=true, to_apply=%region_7.0 | all-reduce | flops 1024 | bytes 8192 | tf_op jit(solution)/shard_map/pmax | solution.py:20
  216.4 4.4 exponential_reduce_fusion.4
  220.7 12.4 %psum.57 = f32[1024]{0:T(1024)S(1)} all-reduce(f32[1024]{0:T(1024)S(1)} %exponential_reduce_fusion.4), channel_id=1, replica_groups=mesh['noise'=8,'sample'=32] {'noise'}, use_global_device_ids=true, to_apply=%region_9.0 | all-reduce | flops 1024 | bytes 8192 | tf_op jit(solution)/shard_map/psum | solution.py:21
  233.2 4.0 subtract_reduce_fusion.3
  237.2 72.8 %pmax.44 = f32[2048]{0:T(1024)S(1)} all-reduce(f32[2048]{0:T(1024)S(1)} %subtract_reduce_fusion.3), channel_id=1, replica_groups=mesh['noise'=8,'sample'=32] {'sample'}, use_global_device_ids=true, to_apply=%region_11.0 | all-reduce | flops 2048 | bytes 16384 | tf_op jit(solution)/shard_map/pmax | solution.py:13
  310.0 4.3 exponential_reduce_fusion.3
  314.3 70.6 %psum.58 = f32[2048]{0:T(1024)S(1)} all-reduce(f32[2048]{0:T(1024)S(1)} %exponential_reduce_fusion.3), channel_id=1, replica_groups=mesh['noise'=8,'sample'=32] {'sample'}, use_global_device_ids=true, to_apply=%region_13.0 | all-reduce | flops 2048 | bytes 16384 | tf_op jit(solution)/shard_map/psum | solution.py:14
  385.0 4.0 subtract_reduce_fusion.2
  389.0 11.9 %pmax.45 = f32[1024]{0:T(1024)S(1)} all-reduce(f32[1024]{0:T(1024)S(1)} %subtract_reduce_fusion.2), channel_id=1, replica_groups=mesh['noise'=8,'sample'=32] {'noise'}, use_global_device_ids=true, to_apply=%region_15.0 | all-reduce | flops 1024 | bytes 8192 | tf_op jit(solution)/shard_map/pmax | solution.py:20
  400.8 4.4 exponential_reduce_fusion.2
  405.2 12.9 %psum.59 = f32[1024]{0:T(1024)S(1)} all-reduce(f32[1024]{0:T(1024)S(1)} %exponential_reduce_fusion.2), channel_id=1, replica_groups=mesh['noise'=8,'sample'=32] {'noise'}, use_global_device_ids=true, to_apply=%region_17.0 | all-reduce | flops 1024 | bytes 8192 | tf_op jit(solution)/shard_map/psum | solution.py:21
  418.1 4.0 subtract_reduce_fusion.1
  422.1 72.8 %pmax.46 = f32[2048]{0:T(1024)S(1)} all-reduce(f32[2048]{0:T(1024)S(1)} %subtract_reduce_fusion.1), channel_id=1, replica_groups=mesh['noise'=8,'sample'=32] {'sample'}, use_global_device_ids=true, to_apply=%region_19.0 | all-reduce | flops 2048 | bytes 16384 | tf_op jit(solution)/shard_map/pmax | solution.py:13
  494.9 4.3 exponential_reduce_fusion.1
  499.3 70.8 %psum.60 = f32[2048]{0:T(1024)S(1)} all-reduce(f32[2048]{0:T(1024)S(1)} %exponential_reduce_fusion.1), channel_id=1, replica_groups=mesh['noise'=8,'sample'=32] {'sample'}, use_global_device_ids=true, to_apply=%region_21.0 | all-reduce | flops 2048 | bytes 16384 | tf_op jit(solution)/shard_map/psum | solution.py:14
  570.1 0.0 copy-start
  570.1 4.0 subtract_reduce_fusion
  574.1 11.9 %pmax.47 = f32[1024]{0:T(1024)S(1)} all-reduce(f32[1024]{0:T(1024)S(1)} %subtract_reduce_fusion), channel_id=1, replica_groups=mesh['noise'=8,'sample'=32] {'noise'}, use_global_device_ids=true, to_apply=%region_23.0 | all-reduce | flops 1024 | bytes 8192 | tf_op jit(solution)/shard_map/pmax | solution.py:20
  586.0 4.4 exponential_reduce_fusion
  590.3 12.9 %psum.61 = f32[1024]{0:T(1024)S(1)} all-reduce(f32[1024]{0:T(1024)S(1)} %exponential_reduce_fusion), channel_id=1, replica_groups=mesh['noise'=8,'sample'=32] {'noise'}, use_global_device_ids=true, to_apply=%region_25.0 | all-reduce | flops 1024 | bytes 8192 | tf_op jit(solution)/shard_map/psum | solution.py:21
  603.3 0.0 copy-start.1
  603.3 6.5 fusion.2
  609.8 0.0 all-reduce.2.cloned.1.call-update
  609.8 0.0 copy-done
  609.8 0.0 copy-done.1
  609.8 4.3 fusion
  614.1 72.9 %psum.63 = f32[2048]{0:T(1024)S(1)} all-reduce(f32[2048]{0:T(1024)S(1)} %fusion), channel_id=1, replica_groups=mesh['noise'=8,'sample'=32] {'sample'}, use_global_device_ids=true, to_apply=%region_28.0 | all-reduce | flops 2048 | bytes 16384 | tf_op jit(solution)/shard_map/psum | solution.py:64
  687.0 0.1 dynamic_slice.7
  687.1 72.8 %all-reduce.2.cloned.1.call-done = f32[2048,256]{1,0:T(8,128)} async-done(((f32[2048,256]{1,0:T(8,128)}), f32[2048,256]{1,0:T(8,128)}) %all-reduce.2.cloned.1.call-update) | async-done | bytes 2097168 | tf_op jit(solution)/shard_map/psum | solution.py:64
  759.9 1.5 divide_convert_fusion
  (6 shorter events, 0.1 us)
Async XLA Ops:
  9.0 40.1 %all-to-all-start = ((bf16[32,64,256]{2,1,0:T(8,128)(2,1)}), bf16[32,64,256]{2,1,0:T(8,128)(2,1)S(1)}, u32[]{:S(2)}, u32[]{:S(2)}) async-start(bf16[32,64,256]{2,1,0:T(8,128)(2,1)} %stack.2), calls=%async_computation | async-start | bytes 2097152 | tf_op jit(solution)/shard_map/all_to_all | solution.py:27
  20.5 739.4 %all-reduce.2.cloned.1.call-start = ((), (), s32[]{:S(2)}) async-start(), calls=%async_computation.1 | async-start | bytes 4194304 | tf_op jit(solution)/shard_map/psum | solution.py:64
  570.1 39.7 %copy-start = (f32[2048]{0:T(1024)}, f32[2048]{0:T(1024)S(1)}, u32[]{:S(2)}) copy-start(f32[2048]{0:T(1024)S(1)} %add_subtract_fusion) | copy-start | bytes 24580
  603.3 6.5 copy-start.1
Sparse Core Ops, SparseCore 0:
  609.9 149.9 all-reduce.1
